TPU v7x, 128 devices: a whole 4x4x4 slice. The times are simulated.
128 devices in a mesh: rows: 64 (over y, z_hi, x, core), frames: 2 (over z_lo).
Axes of the slice: x: 4, y: 4, z: 4 (z_hi: 2, z_lo: 2; z = z_hi * 2 + z_lo), core: 2. Of those that a mesh axis runs over, the one named last changes fastest.
Arguments:
- video: bfloat16 [8, 768, 512, 128], P('frames', 'rows'), may hold values from -6 to 6
- spatial_kernel: bfloat16 [3, 3, 128, 128], replicated, may hold values from -0.1875 to 0.1875
- spatial_bias: float32 [128], replicated, may hold values from -3 to 3
- temporal_kernel: bfloat16 [3, 128, 128], replicated, may hold values from -0.3125 to 0.3125
- temporal_bias: float32 [128], replicated, may hold values from -3 to 3
Outputs:
- doubled: bfloat16 [16, 768, 512, 128], P('frames', None, 'rows')
All inputs are finite; a program needn't handle non-finite values.
Results may differ from a plain program's by a relative error of at most 0.0052.
Values may be sent and summed in bfloat16 or wider, within the bound.
A program may use at most 192 MiB of HBM per device.

v0:
```python
import jax
import jax.numpy as jnp
from jax import lax
from jax.sharding import PartitionSpec as P

FRAMES = 8


def extended_2(block, sides, width):
    for axis, dim in sides:
        count = lax.axis_size(axis)
        forward = [(i, i + 1) for i in range(count - 1)]
        backward = [(target, source) for source, target in forward]
        low = lax.ppermute(
            lax.slice_in_dim(block, block.shape[dim] - width, None, axis=dim), axis, forward
        )
        high = lax.ppermute(lax.slice_in_dim(block, 0, width, axis=dim), axis, backward)
        block = jnp.concatenate([low, block, high], axis=dim)
    return block


def temporal_section(extended, first_frame, temporal_kernel, temporal_bias):
    count = extended.shape[0] - 2
    widened = extended.astype(jnp.float32)
    middles = (widened[:-1] + widened[1:]) * 0.5
    shape_tail = (1,) * (extended.ndim - 1)
    global_index = (first_frame - 1 + jnp.arange(count + 1, dtype=jnp.int32)).reshape(
        (count + 1,) + shape_tail
    )
    middles = jnp.where(global_index == FRAMES - 1, widened[:-1], middles)
    middles = jnp.where(global_index < 0, 0.0, middles)
    upsampled = (
        jnp.stack([middles, widened[1:]], axis=1)
        .reshape((2 * count + 2,) + extended.shape[1:])
        .astype(jnp.bfloat16)
    )
    total = upsampled[1 : 1 + 2 * count].astype(jnp.float32) + temporal_bias
    for shift in range(3):
        total = total + jnp.einsum(
            "thwc,cd->thwd",
            upsampled[shift : shift + 2 * count],
            temporal_kernel[shift],
            preferred_element_type=jnp.float32,
        )
    return total.astype(jnp.bfloat16)


def per_device(video, spatial_kernel, spatial_bias, temporal_kernel, temporal_bias):
    local_frames = video.shape[0]
    first_frame = lax.axis_index("frames") * local_frames
    rimmed = extended_2(video, (("rows", 1),), 1)
    spatial = lax.conv_general_dilated(
        rimmed,
        spatial_kernel,
        (1, 1),
        ((0, 0), (1, 1)),
        dimension_numbers=("NHWC", "HWIO", "NHWC"),
        preferred_element_type=jnp.float32,
    )
    spatial = (spatial + spatial_bias).astype(jnp.bfloat16)
    extended = extended_2(spatial, (("frames", 0),), 1)
    result = temporal_section(extended, first_frame, temporal_kernel, temporal_bias)
    return lax.all_to_all(result, "rows", split_axis=2, concat_axis=1, tiled=True)


def solution(mesh):
    placed = (P("frames", "rows", None, None), P(), P(), P(), P())
    return jax.shard_map(
        per_device,
        mesh=mesh,
        in_specs=placed,
        out_specs=P("frames", None, "rows", None),
        check_vma=False,
    )
```

profile of v0, /device:TPU:1, one launch (start us, length us, event | category | flops | bytes accessed | tf_op | source)
XLA Modules:
  0.0 425.9 jit_solution(16639808916128554681)
XLA Ops:
  1.3 4.5 %collective-permute-start = (bf16[4,1,512,128]{3,2,1,0:T(8,128)(2,1)S(1)}, bf16[4,1,512,128]{3,2,1,0:T(8,128)(2,1)S(1)}, u32[]{:S(2)}, u32[]{:S(2)}) collective-permute-start(bf16[4,1,512,128]{3,2,1,0:T(8,128)(2,1)S(1)} %get-tuple-element.9), channel_id=1, source_target_pairs={{0,2},{2,4},{4,6},{6,8},{8,10},{10,12},{12,14},{14,16},{16,18},{18... | collective-permute-start | bytes 1572872 | tf_op jit(solution)/shard_map/ppermute | solution.py:14
  7.8 4.2 collective-permute-done
  11.9 4.4 %collective-permute-done.1 = bf16[4,1,512,128]{3,2,1,0:T(8,128)(2,1)S(1)} collective-permute-done((bf16[4,1,512,128]{3,2,1,0:T(8,128)(2,1)S(1)}, bf16[4,1,512,128]{3,2,1,0:T(8,128)(2,1)S(1)}, u32[]{:S(2)}, u32[]{:S(2)}) %collective-permute-start.1) | collective-permute-done | bytes 524320 | tf_op jit(solution)/shard_map/ppermute | solution.py:17
  16.3 6.3 %maximum_bitcast_fusion = bf16[14,4,512,128]{3,2,0,1:T(8,128)(2,1)} fusion(bf16[4,1,512,128]{3,2,1,0:T(8,128)(2,1)S(1)} %collective-permute-done.1, bf16[4,12,512,128]{3,2,1,0:T(8,128)(2,1)} %param.5, bf16[4,1,512,128]{3,2,1,0:T(8,128)(2,1)S(1)} %collective-permute-done), kind=kLoop, calls=%fused_computation.19 | loop fusion | flops 7340032 | bytes 14680064 | tf_op jit(solution)/shard_map/concatenate | solution.py:18
  22.7 12.0 %copy.36 = bf16[14,4,512,128]{3,1,2,0:T(4,128)(2,1)} copy(bf16[14,4,512,128]{3,2,0,1:T(8,128)(2,1)} %maximum_bitcast_fusion) | data formatting | bytes 14680064
  34.7 9.0 %pad.clone = bf16[14,4,520,128]{3,1,2,0:T(4,128)(2,1)} pad(bf16[14,4,512,128]{3,1,2,0:T(4,128)(2,1)} %copy.36, bf16[]{:T(256)} %constant.18), padding=0_0x0_0x1_7x0_0 | pad | bytes 14794754 | tf_op jit(solution)/shard_map/concatenate | solution.py:18
  44.8 5.4 %fusion.5 = bf16[14,4,8,67,128]{4,1,3,2,0:T(4,128)(2,1)S(1)} fusion(bf16[14,4,7,2,128]{4,1,3,2,0:T(4,128)(2,1)S(1)} %slice.61, bf16[14,4,8,65,128]{4,1,3,2,0:T(4,128)(2,1)} %bitcast.51), kind=kLoop, calls=%fused_computation.16 | loop fusion | flops 23052288 | bytes 15339520 | tf_op jit(solution)/shard_map/conv_general_dilated | solution.py:52
  50.2 15.7 %add_convert_fusion.1 = bf16[12,32,65,128]{3,1,2,0:T(8,128)(2,1)S(1)} fusion(bf16[3,3,128,128]{3,2,1,0:T(8,128)(2,1)S(1)} %copy-done, bf16[14,4,8,67,128]{4,1,3,2,0:T(4,128)(2,1)S(1)} %fusion.5, f32[128]{0:T(128)S(1)} %copy-done.6, pred[32,65]{0,1:T(8,128)(4,1)S(1)} %copy-done.7), kind=kOutput, calls=%fused_computation.10 | convolution fusion | flops 7370588160 | bytes 14371360 | tf_op jit(solution)/shard_map/conv_general_dilated | solution.py:52
  65.9 5.6 %copy.27 = bf16[12,32,65,128]{3,2,1,0:T(8,128)(2,1)} copy(bf16[12,32,65,128]{3,1,2,0:T(8,128)(2,1)S(1)} %add_convert_fusion.1) | data formatting | bytes 12779520 | tf_op jit(solution)/shard_map/convert_element_type | solution.py:60
  71.5 10.2 %reshape.23 = bf16[12,4,520,128]{3,2,1,0:T(8,128)(2,1)} reshape(bf16[12,32,65,128]{3,2,1,0:T(8,128)(2,1)} %copy.27) | data formatting | bytes 12779520 | tf_op jit(solution)/shard_map/convert_element_type | solution.py:60
  94.4 26.9 %collective-permute-done.2 = bf16[1,12,512,128]{3,2,0,1:T(8,128)(2,1)S(1)} collective-permute-done((bf16[1,12,512,128]{3,2,0,1:T(8,128)(2,1)}, bf16[1,12,512,128]{3,2,0,1:T(8,128)(2,1)S(1)}, u32[]{:S(2)}, u32[]{:S(2)}) %collective-permute-start.2) | collective-permute-done | bytes 1572896 | tf_op jit(solution)/shard_map/ppermute | solution.py:14
  125.3 10.6 %maximum_convert_fusion = f32[6,12,512,128]{3,2,0,1:T(8,128)} fusion(bf16[1,12,512,128]{3,2,0,1:T(8,128)(2,1)S(1)} %collective-permute-done.3, bf16[4,12,512,128]{3,2,0,1:T(8,128)(2,1)} %copy-done.3, bf16[1,12,512,128]{3,2,0,1:T(8,128)(2,1)S(1)} %collective-permute-done.2), kind=kLoop, calls=%fused_computation.13 | loop fusion | flops 14155776 | bytes 28311552 | tf_op jit(solution)/shard_map/convert_element_type | solution.py:24
  136.0 10.0 %fusion.3 = bf16[5,1,12,512,128]{4,3,0,2,1:T(8,128)(2,1)} fusion(f32[6,12,512,128]{3,2,0,1:T(8,128)} %maximum_convert_fusion), kind=kLoop, calls=%fused_computation.14 | loop fusion | bytes 15728640 | tf_op jit(solution)/shard_map/stack | solution.py:33
  146.0 11.2 %fusion.4 = bf16[5,1,12,512,128]{4,3,0,2,1:T(8,128)(2,1)S(1)} fusion(f32[6,12,512,128]{3,2,0,1:T(8,128)} %maximum_convert_fusion, pred[5]{0:T(512)(128)(4,1)S(1)} %get-tuple-element.11, pred[5]{0:T(512)(128)(4,1)S(1)} %get-tuple-element.12), kind=kLoop, calls=%fused_computation.15 | loop fusion | flops 19660800 | bytes 39321608 | tf_op jit(solution)/shard_map/stack | solution.py:33
  159.8 8.8 %fusion.1 = (bf16[4,2,12,512,128]{4,3,0,2,1:T(8,128)(2,1)}, bf16[4,2,12,512,128]{4,3,0,2,1:T(8,128)(2,1)}) fusion(bf16[5,1,12,512,128]{4,3,0,2,1:T(8,128)(2,1)S(1)} %fusion.4, bf16[5,1,12,512,128]{4,3,0,2,1:T(8,128)(2,1)S(1)} %copy-done.2), kind=kLoop, calls=%fused_computation.11 | loop fusion | flops 12582912 | bytes 40894464 | tf_op jit(solution)/shard_map/stack | solution.py:33
  168.5 7.8 %copy.28 = bf16[5,2,12,512,128]{4,3,2,1,0:T(8,128)(2,1)} copy(bf16[5,2,12,512,128]{4,3,0,2,1:T(8,128)(2,1)S(1)} %pad_maximum_fusion) | data formatting | bytes 31457280 | tf_op jit(solution)/shard_map/stack | solution.py:33
  176.3 6.5 %copy.29 = bf16[4,2,12,512,128]{4,3,2,1,0:T(8,128)(2,1)S(1)} copy(bf16[4,2,12,512,128]{4,3,0,2,1:T(8,128)(2,1)} %get-tuple-element.5) | data formatting | bytes 25165824 | tf_op jit(solution)/shard_map/slice | solution.py:41
  182.9 5.8 %copy.30 = bf16[4,2,12,512,128]{4,3,2,1,0:T(8,128)(2,1)} copy(bf16[4,2,12,512,128]{4,3,0,2,1:T(8,128)(2,1)S(1)} %bitcast.49) | data formatting | bytes 25165824 | tf_op jit(solution)/shard_map/slice | solution.py:41
  188.7 10.0 %fusion.11 = f32[8,12,512,128]{3,2,1,0:T(8,128)} fusion(bf16[8,12,512,128]{3,2,1,0:T(8,128)(2,1)S(1)} %bitcast.44, bf16[3,128,128]{2,1,0:T(8,128)(2,1)S(1)} %copy-done.4), kind=kOutput, calls=%fused_computation.24 | convolution fusion | flops 1610612736 | bytes 37781504 | tf_op jit(solution)/shard_map/thwc,cd->thwd/dot_general | solution.py:39
  198.7 12.8 %fusion.8 = f32[8,12,512,128]{3,2,1,0:T(8,128)} fusion(bf16[8,12,512,128]{3,2,1,0:T(8,128)(2,1)} %bitcast.45, bf16[3,128,128]{2,1,0:T(8,128)(2,1)S(1)} %copy-done.4), kind=kOutput, calls=%fused_computation.21 | convolution fusion | flops 1610612736 | bytes 37781504 | tf_op jit(solution)/shard_map/thwc,cd->thwd/dot_general | solution.py:39
  211.5 29.2 %add_convert_fusion = bf16[8,12,512,128]{3,2,1,0:T(8,128)(2,1)} fusion(f32[8,12,512,128]{3,2,1,0:T(8,128)} %fusion.8, f32[8,12,512,128]{3,2,1,0:T(8,128)} %fusion.11, bf16[10,12,512,128]{3,2,1,0:T(8,128)(2,1)} %bitcast.46, f32[128]{0:T(128)S(1)} %copy-done.5, bf16[3,128,128]{2,1,0:T(8,128)(2,1)S(1)} %copy-done.4), kind=kOutput, calls=%fused_computation | convolution fusion | flops 1648361472 | bytes 91259392 | tf_op jit(solution)/shard_map/thwc,cd->thwd/dot_general | solution.py:39
  240.7 11.5 %copy.31 = bf16[8,12,512,128]{3,0,1,2:T(8,128)(2,1)S(1)} copy(bf16[8,12,512,128]{3,2,1,0:T(8,128)(2,1)} %add_convert_fusion) | data formatting | bytes 25165824 | tf_op jit(solution)/shard_map/convert_element_type | solution.py:45
  252.2 159.4 %all_to_all.18 = bf16[8,12,512,128]{3,0,1,2:T(8,128)(2,1)S(1)} all-to-all(bf16[8,12,512,128]{3,0,1,2:T(8,128)(2,1)S(1)} %copy.31), channel_id=1, replica_groups=mesh['rows'=64,'frames'=2] {'rows'}, dimensions={2} | all-to-all | bytes 25165824 | tf_op jit(solution)/shard_map/all_to_all | solution.py:63
  411.6 14.3 %copy.32 = bf16[8,64,12,8,128]{4,3,2,1,0:T(8,128)(2,1)} copy(bf16[8,64,12,8,128]{4,0,2,3,1:T(8,128)(2,1)S(1)} %bitcast.47) | data formatting | bytes 25165824 | tf_op jit(solution)/shard_map/all_to_all | solution.py:63
  (33 shorter events, 23.6 us)
Async XLA Ops:
  0.0 50.1 %copy-start = (bf16[3,3,128,128]{3,2,1,0:T(8,128)(2,1)S(1)}, bf16[3,3,128,128]{3,2,1,0:T(8,128)(2,1)}, u32[]{:S(2)}) copy-start(bf16[3,3,128,128]{3,2,1,0:T(8,128)(2,1)} %param.6) | copy-start | bytes 884740
  1.3 10.6 %collective-permute-start = (bf16[4,1,512,128]{3,2,1,0:T(8,128)(2,1)S(1)}, bf16[4,1,512,128]{3,2,1,0:T(8,128)(2,1)S(1)}, u32[]{:S(2)}, u32[]{:S(2)}) collective-permute-start(bf16[4,1,512,128]{3,2,1,0:T(8,128)(2,1)S(1)} %get-tuple-element.9), channel_id=1, source_target_pairs={{0,2},{2,4},{4,6},{6,8},{8,10},{10,12},{12,14},{14,16},{16,18},{18... | collective-permute-start | bytes 1572872 | tf_op jit(solution)/shard_map/ppermute | solution.py:14
  5.8 10.5 %collective-permute-start.1 = (bf16[4,1,512,128]{3,2,1,0:T(8,128)(2,1)S(1)}, bf16[4,1,512,128]{3,2,1,0:T(8,128)(2,1)S(1)}, u32[]{:S(2)}, u32[]{:S(2)}) collective-permute-start(bf16[4,1,512,128]{3,2,1,0:T(8,128)(2,1)S(1)} %get-tuple-element.10), channel_id=1, source_target_pairs={{2,0},{4,2},{6,4},{8,6},{10,8},{12,10},{14,12},{16,14},{18,16},{20... | collective-permute-start | bytes 1572872 | tf_op jit(solution)/shard_map/ppermute | solution.py:17
  34.7 15.5 %copy-start.6 = (f32[128]{0:T(128)S(1)}, f32[128]{0:T(128)}, u32[]{:S(2)}) copy-start(f32[128]{0:T(128)} %param.7) | copy-start | bytes 1540
  34.7 15.5 %copy-start.7 = (pred[32,65]{0,1:T(8,128)(4,1)S(1)}, pred[32,65]{0,1:T(8,128)(4,1)}, u32[]{:S(2)}) copy-start(pred[32,65]{0,1:T(8,128)(4,1)} %constant.22) | copy-start | bytes 6244
  84.8 2.7 copy-start.3
  89.4 31.8 %collective-permute-start.2 = (bf16[1,12,512,128]{3,2,0,1:T(8,128)(2,1)}, bf16[1,12,512,128]{3,2,0,1:T(8,128)(2,1)S(1)}, u32[]{:S(2)}, u32[]{:S(2)}) collective-permute-start(bf16[1,12,512,128]{3,2,0,1:T(8,128)(2,1)} %get-tuple-element.7), channel_id=1, source_target_pairs={{0,1},{2,3},{4,5},{6,7},{8,9},{10,11},{12,13},{14,15},{16,17},{18,... | collective-permute-start | bytes 4718600 | tf_op jit(solution)/shard_map/ppermute | solution.py:14
  93.0 32.3 %collective-permute-start.3 = (bf16[1,12,512,128]{3,2,0,1:T(8,128)(2,1)}, bf16[1,12,512,128]{3,2,0,1:T(8,128)(2,1)S(1)}, u32[]{:S(2)}, u32[]{:S(2)}) collective-permute-start(bf16[1,12,512,128]{3,2,0,1:T(8,128)(2,1)} %get-tuple-element.8), channel_id=1, source_target_pairs={{1,0},{3,2},{5,4},{7,6},{9,8},{11,10},{13,12},{15,14},{17,16},{19,... | collective-permute-start | bytes 4718600 | tf_op jit(solution)/shard_map/ppermute | solution.py:17
  146.0 12.2 %copy-start.2 = (bf16[5,1,12,512,128]{4,3,0,2,1:T(8,128)(2,1)S(1)}, bf16[5,1,12,512,128]{4,3,0,2,1:T(8,128)(2,1)}, u32[]{:S(2)}) copy-start(bf16[5,1,12,512,128]{4,3,0,2,1:T(8,128)(2,1)} %fusion.3) | copy-start | bytes 23592964
  168.5 14.4 %slice-start = ((s8[12582912]{0:T(1024)(128)(4,1)}), s8[4194304]{0:T(1024)(128)(4,1)S(1)}, s32[]{:S(2)}) async-start(s8[12582912]{0:T(1024)(128)(4,1)} %bitcast.48), calls=%async_computation.1 | async-start | bytes 8388608
  168.5 14.4 %slice-start.1 = ((s8[12582912]{0:T(1024)(128)(4,1)}), s8[4194304]{0:T(1024)(128)(4,1)S(1)}, s32[]{:S(2)}) async-start(s8[12582912]{0:T(1024)(128)(4,1)} %bitcast.48), calls=%async_computation.2 | async-start | bytes 8388608
  176.3 6.6 %slice-start.2 = ((s8[12582912]{0:T(1024)(128)(4,1)}), s8[4194304]{0:T(1024)(128)(4,1)S(1)}, s32[]{:S(2)}) async-start(s8[12582912]{0:T(1024)(128)(4,1)} %bitcast.48), calls=%async_computation.3 | async-start | bytes 8388608
  182.9 5.8 %copy-start.4 = (bf16[3,128,128]{2,1,0:T(8,128)(2,1)S(1)}, bf16[3,128,128]{2,1,0:T(8,128)(2,1)}, u32[]{:S(2)}) copy-start(bf16[3,128,128]{2,1,0:T(8,128)(2,1)} %param.8) | copy-start | bytes 294916
  198.7 12.8 %copy-start.5 = (f32[128]{0:T(128)S(1)}, f32[128]{0:T(128)}, u32[]{:S(2)}) copy-start(f32[128]{0:T(128)} %param.9) | copy-start | bytes 1540
  411.6 14.3 %copy-start.1 = (bf16[3,3,128,128]{3,2,1,0:T(8,128)(2,1)S(1)}, bf16[3,3,128,128]{3,2,1,0:T(8,128)(2,1)}, u32[]{:S(2)}) copy-start(bf16[3,3,128,128]{3,2,1,0:T(8,128)(2,1)} %param.6) | copy-start | bytes 884740
where the time goes:
time: 427 us; the launch traced here: 426 us
  blocking collectives  159 us (37%)
  local copies, waits for them, and re-layouts  104 us (24%)
  matrix products  67.7 us (16%)
  other arithmetic  43.9 us (10%)
  waiting for transfers between devices  39.5 us (9%)
  starting transfers between devices  11.4 us (3%)
    all_to_all x1, blocking collectives, per_device(): lax.all_to_all(result, 'rows', split_axis=2, concat_axis=1, tiled=True)  159 us
    dot_general x3, matrix products, temporal_section(): jnp.einsum('thwc,cd->thwd', upsampled[shift:shift + 2 * count], temporal_...  52 us
    ppermute x2, waiting for transfers between devices, extended_2(): lax.ppermute(lax.slice_in_dim(block, block.shape[dim] - width, None, axis...  31 us
    another operation x3, other arithmetic, temporal_section(): jnp.stack([middles, widened[1:]], axis=1)  21.5 us
    convert_element_type x3, local copies, waits for them, and re-layouts, per_device(): spatial = (spatial + spatial_bias).astype(jnp.bfloat16)  18.9 us
    another operation x2, local copies, waits for them, and re-layouts, temporal_section(): jnp.stack([middles, widened[1:]], axis=1)  17.8 us
    unnamed x23, local copies, waits for them, and re-layouts  15.8 us
    conv_general_dilated x1, matrix products, per_device(): lax.conv_general_dilated(rimmed, spatial_kernel, (1, 1), ((0, 0), (1, 1))...  15.7 us
  transfers between devices with their start and end apart: 4, of which 4 were waited for; matrix products, arithmetic and copies ran while one was open for 0% of the time, Pallas kernels for 0%

commit v1 on v0

v1 whole, which is shorter than its diff:
```python
import jax
import jax.numpy as jnp
from jax import lax
from jax.experimental import pallas as pl
from jax.experimental.pallas import tpu as pltpu
from jax.sharding import PartitionSpec as P

MESH = pl.DeviceIdType.MESH
C = 128
F = 4
R = 12
W = 512
N = 64
COLS = W // N
BLOCK = R * COLS
TILE = 768


def partner(row, step):
    dx = step % 4
    dy = (step // 4 + step) % 4
    dw = (step // 16 + step) % 4
    y = (row // 16 + dy) % 4
    z = (row // 8 + dw // 2) % 2
    x = (row // 2 + dx) % 4
    core = (row + dw) % 2
    return ((y * 2 + z) * 4 + x) * 2 + core


def spatial_kernel_body(
    video, taps, bias, received, rows, left, right, outgoing, weights,
    load_sem, rim_send, rim_recv, send_sem, recv_sem, own_sem,
):
    me = lax.axis_index("rows")
    side = lax.axis_index("frames")
    barrier = pltpu.get_barrier_semaphore()

    @pl.loop(0, N)
    def _(step):
        peer = partner(me, step)

        @pl.when(step > 0)
        def _():
            pl.semaphore_signal(barrier, inc=1, device_id=(peer, side), device_id_type=MESH)

        pl.semaphore_signal(barrier, inc=1, device_id=(peer, 1 - side), device_id_type=MESH)

    def frame_at(step):
        return (step + 3 * (1 - side)) % F

    def load(frame):
        return pltpu.make_async_copy(video.at[frame], rows.at[frame, pl.ds(1, R)], load_sem.at[frame])

    for step in range(F):
        load(frame_at(step)).start()

    for b in range(3):
        for j in range(4):
            for o in range(2):
                a = j - o
                block = taps[a, b] if 0 <= a < 3 else jnp.zeros((C, C), jnp.bfloat16)
                weights[pl.ds((b * 4 + j) * C, C), pl.ds(o * C, C)] = block

    pl.semaphore_wait(barrier, 2 * N - 1)

    def rim_copies(frame):
        up = pltpu.make_async_remote_copy(
            src_ref=video.at[frame, 0], dst_ref=rows.at[frame, R + 1],
            send_sem=rim_send.at[frame, 0], recv_sem=rim_recv.at[frame, 0],
            device_id=((me + N - 1) % N, side), device_id_type=MESH,
        )
        down = pltpu.make_async_remote_copy(
            src_ref=video.at[frame, R - 1], dst_ref=rows.at[frame, 0],
            send_sem=rim_send.at[frame, 1], recv_sem=rim_recv.at[frame, 1],
            device_id=((me + 1) % N, side), device_id_type=MESH,
        )
        return up, down

    for step in range(F):
        for copy in rim_copies(frame_at(step)):
            copy.start()

    column = lax.broadcasted_iota(jnp.int32, (W, C), 0)

    @pl.loop(0, F)
    def _(step):
        frame = frame_at(step)
        load(frame).wait()
        for copy in rim_copies(frame):
            copy.wait()

        @pl.when(me == 0)
        def _():
            rows[frame, 0] = jnp.zeros((W, C), jnp.bfloat16)

        @pl.when(me == N - 1)
        def _():
            rows[frame, R + 1] = jnp.zeros((W, C), jnp.bfloat16)

        @pl.loop(0, R + 2)
        def _(i):
            row = rows[frame, i].astype(jnp.float32)
            left[i] = jnp.where(column == 0, 0.0, pltpu.roll(row, 1, 0)).astype(jnp.bfloat16)
            right[i] = jnp.where(column == W - 1, 0.0, pltpu.roll(row, W - 1, 0)).astype(jnp.bfloat16)

        @pl.loop(0, R // 2)
        def _(pair):
            first = 2 * pair
            pieces = (
                [left[first + j] for j in range(4)]
                + [rows[frame, first + j] for j in range(4)]
                + [right[first + j] for j in range(4)]
            )
            total = jnp.dot(
                jnp.concatenate(pieces, axis=1), weights[...], preferred_element_type=jnp.float32
            )
            upper = (total[:, :C] + bias[...]).reshape(N, COLS, C)
            lower = (total[:, C:] + bias[...]).reshape(N, COLS, C)
            both = jnp.concatenate([upper, lower], axis=1).astype(jnp.bfloat16)
            outgoing[frame, :, pl.ds(pl.multiple_of(pair * 2 * COLS, 2 * COLS), 2 * COLS), :] = both

        pltpu.make_async_copy(
            outgoing.at[frame, me], received.at[frame, me], own_sem.at[frame]
        ).start()

        @pl.loop(0, N)
        def _(index):
            peer = partner(me, index)

            @pl.when(index > 0)
            def _():
                pltpu.make_async_remote_copy(
                    src_ref=outgoing.at[frame, peer], dst_ref=received.at[frame, me],
                    send_sem=send_sem.at[frame], recv_sem=recv_sem.at[frame],
                    device_id=(peer, side), device_id_type=MESH,
                ).start()

            @pl.when(step == 0)
            def _():
                pltpu.make_async_remote_copy(
                    src_ref=outgoing.at[frame, peer], dst_ref=received.at[F, me],
                    send_sem=send_sem.at[F], recv_sem=recv_sem.at[F],
                    device_id=(peer, 1 - side), device_id_type=MESH,
                ).start()

    def whole(slot, count, sem):
        part = received.at[slot, pl.ds(0, count)]
        return pltpu.make_async_copy(part, part, sem.at[slot])

    for frame in range(F):
        whole(frame, N - 1, send_sem).wait()
        whole(frame, N - 1, recv_sem).wait()
        pltpu.make_async_copy(
            outgoing.at[frame, me], received.at[frame, me], own_sem.at[frame]
        ).wait()
    whole(F, N, send_sem).wait()
    whole(F, N, recv_sem).wait()


def spatial_exchange(video, taps, bias):
    return pl.pallas_call(
        spatial_kernel_body,
        out_shape=jax.ShapeDtypeStruct((F + 1, N, BLOCK, C), jnp.bfloat16),
        in_specs=[
            pl.BlockSpec(memory_space=pl.ANY),
            pl.BlockSpec(memory_space=pltpu.VMEM),
            pl.BlockSpec(memory_space=pltpu.VMEM),
        ],
        out_specs=pl.BlockSpec(memory_space=pl.ANY),
        scratch_shapes=[
            pltpu.VMEM((F, R + 2, W, C), jnp.bfloat16),
            pltpu.VMEM((R + 2, W, C), jnp.bfloat16),
            pltpu.VMEM((R + 2, W, C), jnp.bfloat16),
            pltpu.VMEM((F, N, BLOCK, C), jnp.bfloat16),
            pltpu.VMEM((12 * C, 2 * C), jnp.bfloat16),
            pltpu.SemaphoreType.DMA((F,)),
            pltpu.SemaphoreType.DMA((F, 2)),
            pltpu.SemaphoreType.DMA((F, 2)),
            pltpu.SemaphoreType.DMA((F + 1,)),
            pltpu.SemaphoreType.DMA((F + 1,)),
            pltpu.SemaphoreType.DMA((F,)),
        ],
        compiler_params=pltpu.CompilerParams(
            collective_id=0, has_side_effects=True, vmem_limit_bytes=48 * 2**20
        ),
        cost_estimate=pl.CostEstimate(
            flops=2 * 9 * C * C * F * R * W, bytes_accessed=9 * R * W * C * 2, transcendentals=0
        ),
        name="spatial_exchange",
    )(video, taps, bias)


def temporal_kernel_body(frames, taps, bias, doubled, weights):
    side = lax.axis_index("frames")

    @pl.when(pl.program_id(0) == 0)
    def _():
        for j in range(4):
            for o in range(2):
                d = j - o
                block = taps[d] if 0 <= d < 3 else jnp.zeros((C, C), jnp.bfloat16)
                weights[pl.ds(j * C, C), pl.ds(o * C, C)] = block

    own = [frames[k].astype(jnp.float32) for k in range(F)]
    halo = frames[F].astype(jnp.float32)
    first_side = side == 0
    zero = jnp.zeros((TILE, C), jnp.float32)
    before = jnp.where(first_side, zero, (halo + own[0]) * 0.5).astype(jnp.bfloat16)
    after = jnp.where(first_side, halo, zero).astype(jnp.bfloat16)
    beyond = jnp.where(first_side, halo, own[F - 1])
    for k in range(F):
        middle = ((own[k] + (own[k + 1] if k + 1 < F else beyond)) * 0.5).astype(jnp.bfloat16)
        following = frames[k + 1] if k + 1 < F else after
        window = jnp.concatenate([before, frames[k], middle, following], axis=1)
        total = jnp.dot(window, weights[...], preferred_element_type=jnp.float32)
        doubled[2 * k] = (total[:, :C] + (own[k] + bias[...])).astype(jnp.bfloat16)
        doubled[2 * k + 1] = (
            total[:, C:] + (middle.astype(jnp.float32) + bias[...])
        ).astype(jnp.bfloat16)
        before = middle


def temporal(frames, taps, bias):
    count = N * BLOCK
    return pl.pallas_call(
        temporal_kernel_body,
        out_shape=jax.ShapeDtypeStruct((2 * F, count, C), jnp.bfloat16),
        grid=(count // TILE,),
        in_specs=[
            pl.BlockSpec((F + 1, TILE, C), lambda i: (0, i, 0)),
            pl.BlockSpec((3, C, C), lambda i: (0, 0, 0)),
            pl.BlockSpec((1, C), lambda i: (0, 0)),
        ],
        out_specs=pl.BlockSpec((2 * F, TILE, C), lambda i: (0, i, 0)),
        scratch_shapes=[pltpu.VMEM((4 * C, 2 * C), jnp.bfloat16)],
        compiler_params=pltpu.CompilerParams(vmem_limit_bytes=48 * 2**20),
        cost_estimate=pl.CostEstimate(
            flops=2 * 3 * C * C * 2 * F * count, bytes_accessed=13 * count * C * 2, transcendentals=0
        ),
        name="temporal",
    )(frames, taps, bias)


def per_device(video, spatial_kernel, spatial_bias, temporal_kernel, temporal_bias):
    received = spatial_exchange(video, spatial_kernel, spatial_bias.reshape(1, C))
    frames = received.reshape(F + 1, N * BLOCK, C)
    doubled = temporal(frames, temporal_kernel, temporal_bias.reshape(1, C))
    return doubled.reshape(2 * F, N * R, COLS, C)


def solution(mesh):
    placed = (P("frames", "rows", None, None), P(), P(), P(), P())
    return jax.shard_map(
        per_device,
        mesh=mesh,
        in_specs=placed,
        out_specs=P("frames", None, "rows", None),
        check_vma=False,
    )
```

time: 427 us -> 126 us (0.30)
  blocking collectives: 159 us -> 0 us
  Pallas kernels: 0 us -> 124 us
  local copies, waits for them, and re-layouts: 104 us -> 1.62 us
  matrix products: 67.7 us -> 0 us
  other arithmetic: 43.9 us -> 0 us
  waiting for transfers between devices: 39.5 us -> 0 us
  starting transfers between devices: 11.4 us -> 0 us
    all_to_all x1 -> x0, blocking collectives: 159 us -> none  [per_device(): lax.all_to_all(result, 'rows', split_axis=2, concat_axis=1, tiled=True)]
    pallas_call x0 -> x2, Pallas kernels: none -> 124 us  [the longest x1 111 us: spatial_exchange(): pl.pallas_call(spatial_kernel_body, out_shape=jax.ShapeDtypeStruct((F + 1...]
    dot_general x3 -> x0, matrix products: 52 us -> none  [temporal_section(): jnp.einsum('thwc,cd->thwd', upsampled[shift:shift + 2 * count], temporal_...]
    ppermute x4 -> x0, waiting for transfers between devices: 39.5 us -> none  [the longest x2 31 us: extended_2(): lax.ppermute(lax.slice_in_dim(block, block.shape[dim] - width, None, axis...]
    convert_element_type x4 -> x0, local copies, waits for them, and re-layouts: 30.4 us -> none  [the longest x3 18.9 us: per_device(): spatial = (spatial + spatial_bias).astype(jnp.bfloat16)]
    another operation x3 -> x0, other arithmetic: 21.5 us -> none  [temporal_section(): jnp.stack([middles, widened[1:]], axis=1)]
    another operation x2 -> x0, local copies, waits for them, and re-layouts: 17.8 us -> none  [temporal_section(): jnp.stack([middles, widened[1:]], axis=1)]
    conv_general_dilated x1 -> x0, matrix products: 15.7 us -> none  [per_device(): lax.conv_general_dilated(rimmed, spatial_kernel, (1, 1), ((0, 0), (1, 1))...]
  transfers between devices with their start and end apart: 4 -> 0, of which waited for: 4 -> 0; matrix products, arithmetic and copies ran while one was open for 0% -> 0% of each run, Pallas kernels for 0% -> 0%
where the time goes in v1:
time: 126 us
  Pallas kernels  124 us (98%)
  local copies, waits for them, and re-layouts  1.62 us (1%)
    pallas_call x1, Pallas kernels, spatial_exchange(): pl.pallas_call(spatial_kernel_body, out_shape=jax.ShapeDtypeStruct((F + 1...  111 us
    pallas_call x1, Pallas kernels, temporal(): pl.pallas_call(temporal_kernel_body, out_shape=jax.ShapeDtypeStruct((2 *...  13 us

profile of v1, /device:TPU:1, one launch (start us, length us, event | category | flops | bytes accessed | tf_op | source)
XLA Modules:
  0.0 126.0 jit_solution(3647359542219645551)
XLA Ops:
  0.0 0.0 copy-start.2
  0.0 1.0 copy-done.2
  1.0 0.0 copy-start.3
  1.0 0.7 copy-done.3
  1.6 0.0 copy-start
  1.6 0.0 copy-start.1
  1.6 111.4 %spatial_exchange.1 = bf16[5,64,96,128]{3,2,1,0:T(8,128)(2,1)} custom-call(bf16[4,12,512,128]{3,2,1,0:T(8,128)(2,1)} %video.1, bf16[3,3,128,128]{3,2,1,0:T(8,128)(2,1)S(1)} %copy-done.2, f32[1,128]{1,0:T(1,128)S(1)} %bitcast.5), custom_call_target="tpu_custom_call" | custom-call | flops 7247757312 | bytes 14155776 | tf_op jit(solution)/shard_map/spatial_exchange/pallas_call | solution.py:161
  113.0 0.0 copy-done
  113.0 0.0 copy-done.1
  113.0 13.0 %temporal.1 = bf16[8,6144,128]{2,1,0:T(8,128)(2,1)} custom-call(bf16[5,6144,128]{2,1,0:T(8,128)(2,1)} %bitcast.6, bf16[3,128,128]{2,1,0:T(8,128)(2,1)S(1)} %copy-done, f32[1,128]{1,0:T(1,128)S(1)} %bitcast.4), custom_call_target="tpu_custom_call" | custom-call | flops 4831838208 | bytes 20447232 | tf_op jit(solution)/shard_map/temporal/pallas_call | solution.py:225
Async XLA Ops:
  0.0 1.0 copy-start.2
  1.0 0.7 copy-start.3
  1.6 111.4 %copy-start = (bf16[3,128,128]{2,1,0:T(8,128)(2,1)S(1)}, bf16[3,128,128]{2,1,0:T(8,128)(2,1)}, u32[]{:S(2)}) copy-start(bf16[3,128,128]{2,1,0:T(8,128)(2,1)} %taps.3) | copy-start | bytes 294916
  1.6 111.4 %copy-start.1 = (f32[128]{0:T(128)S(1)}, f32[128]{0:T(128)}, u32[]{:S(2)}) copy-start(f32[128]{0:T(128)} %param.9) | copy-start | bytes 1540

commit v2 on v0

v2 whole, which is shorter than its diff:
```python
import jax
import jax.numpy as jnp
from jax import lax
from jax.experimental import pallas as pl
from jax.experimental.pallas import tpu as pltpu
from jax.sharding import PartitionSpec as P

MESH = pl.DeviceIdType.MESH
C = 128
F = 4
R = 12
W = 512
N = 64
COLS = W // N
BLOCK = R * COLS
COUNT = N * BLOCK
GROUP = 8
TILE = GROUP * BLOCK
BF16 = jnp.bfloat16
F32 = jnp.float32


def partner(row, step):
    mixed = (37 * step + 10 * step * step) % N
    y = (row // 16 + mixed // 16) % 4
    z = (row // 8 + mixed) % 2
    x = (row // 2 + mixed // 4) % 4
    core = (row + mixed // 2) % 2
    return ((y * 2 + z) * 4 + x) * 2 + core


def spread_taps(taps, weights):
    for j in range(4):
        for o in range(2):
            d = j - o
            block = taps[d] if 0 <= d < 3 else jnp.zeros((C, C), BF16)
            weights[pl.ds(j * C, C), pl.ds(o * C, C)] = block


def two_frames(before, frame, middle, following, weights, bias):
    window = jnp.concatenate([before, frame, middle, following], axis=1)
    total = jnp.dot(window, weights[...], preferred_element_type=F32)
    even = total[:, :C] + (frame.astype(F32) + bias)
    odd = total[:, C:] + (middle.astype(F32) + bias)
    return even.astype(BF16), odd.astype(BF16)


def exchange_body(
    video, spatial_taps, spatial_bias, temporal_taps, temporal_bias,
    received, early,
    rows, left, right, outgoing, weights, time_weights, taps, time_taps, bias, time_bias,
    load_sem, small_sem, rim_send, rim_recv, send_sem, recv_sem, own_sem,
):
    me = lax.axis_index("rows")
    side = lax.axis_index("frames")
    barrier = pltpu.get_barrier_semaphore()

    def frame_at(step):
        return step * (2 * side - 1) + (F - 1) * (1 - side)

    def load(frame):
        return pltpu.make_async_copy(video.at[frame], rows.at[frame, pl.ds(1, R)], load_sem.at[frame])

    load(frame_at(0)).start()
    small = [
        pltpu.make_async_copy(source, target, small_sem.at[k])
        for k, (source, target) in enumerate(
            [(spatial_taps, taps), (spatial_bias, bias), (temporal_taps, time_taps), (temporal_bias, time_bias)]
        )
    ]
    for copy in small:
        copy.start()

    @pl.loop(1, N, unroll=9)
    def _(step):
        peer = lax.rem(me + step, N)
        pl.semaphore_signal(barrier, inc=1, device_id=(peer, side), device_id_type=MESH)
        pl.semaphore_signal(barrier, inc=1, device_id=(peer, 1 - side), device_id_type=MESH)

    pl.semaphore_signal(barrier, inc=1, device_id=(me, 1 - side), device_id_type=MESH)

    for step in range(1, F):
        load(frame_at(step)).start()
    for copy in small:
        copy.wait()
    for b in range(3):
        for j in range(4):
            for o in range(2):
                a = j - o
                block = taps[a, b] if 0 <= a < 3 else jnp.zeros((C, C), BF16)
                weights[pl.ds((b * 4 + j) * C, C), pl.ds(o * C, C)] = block
    spread_taps(time_taps, time_weights)

    def rim_copies(frame):
        up = pltpu.make_async_remote_copy(
            src_ref=video.at[frame, 0], dst_ref=rows.at[frame, R + 1],
            send_sem=rim_send.at[frame, 0], recv_sem=rim_recv.at[frame, 0],
            device_id=((me + N - 1) % N, side), device_id_type=MESH,
        )
        down = pltpu.make_async_remote_copy(
            src_ref=video.at[frame, R - 1], dst_ref=rows.at[frame, 0],
            send_sem=rim_send.at[frame, 1], recv_sem=rim_recv.at[frame, 1],
            device_id=((me + 1) % N, side), device_id_type=MESH,
        )
        return up, down

    def wait_rims(frame):
        for copy in rim_copies(frame):
            copy.wait()

        @pl.when(me == 0)
        def _():
            rows[frame, 0] = jnp.zeros((W, C), BF16)

        @pl.when(me == N - 1)
        def _():
            rows[frame, R + 1] = jnp.zeros((W, C), BF16)

    column = lax.broadcasted_iota(jnp.int32, (W, C), 0)

    def shift(frame, i):
        row = rows[frame, i].astype(F32)
        left[i] = jnp.where(column == 0, 0.0, pltpu.roll(row, 1, 0)).astype(BF16)
        right[i] = jnp.where(column == W - 1, 0.0, pltpu.roll(row, W - 1, 0)).astype(BF16)

    def convolve(frame, pair):
        first = 2 * pair
        pieces = (
            [left[first + j] for j in range(4)]
            + [rows[frame, first + j] for j in range(4)]
            + [right[first + j] for j in range(4)]
        )
        total = jnp.dot(jnp.concatenate(pieces, axis=1), weights[...], preferred_element_type=F32)
        upper = (total[:, :C] + bias[...]).reshape(N, COLS, C)
        lower = (total[:, C:] + bias[...]).reshape(N, COLS, C)
        both = jnp.concatenate([upper, lower], axis=1).astype(BF16)
        outgoing[frame, :, pl.ds(pl.multiple_of(pair * 2 * COLS, 2 * COLS), 2 * COLS), :] = both

    def inner(frame):
        load(frame).wait()
        pl.loop(1, R + 1)(lambda i: shift(frame, i))
        pl.loop(1, R // 2 - 1)(lambda pair: convolve(frame, pair))

    def outer(frame):
        wait_rims(frame)
        pl.loop(0, 2)(lambda k: shift(frame, k * (R + 1)))
        pl.loop(0, 2)(lambda k: convolve(frame, k * (R // 2 - 1)))

    def own(frame):
        return pltpu.make_async_copy(outgoing.at[frame, me], received.at[frame, me], own_sem.at[frame])

    def send(frame, slot, peer, where):
        pltpu.make_async_remote_copy(
            src_ref=outgoing.at[frame, peer], dst_ref=received.at[slot, me],
            send_sem=send_sem.at[slot], recv_sem=recv_sem.at[slot],
            device_id=(peer, where), device_id_type=MESH,
        ).start()

    head = frame_at(0)
    inner(head)
    pl.semaphore_wait(barrier, 2 * N - 1)
    for step in range(F):
        for copy in rim_copies(frame_at(step)):
            copy.start()
    outer(head)
    send(head, F, me, 1 - side)

    @pl.loop(1, N)
    def _(index):
        peer = partner(me, index)
        send(head, head, peer, side)
        send(head, F, peer, 1 - side)

    own(head).start()

    @pl.loop(1, F)
    def _(step):
        frame = frame_at(step)
        inner(frame)
        outer(frame)

        @pl.loop(1, N)
        def _(index):
            send(frame, frame, partner(me, index), side)

        own(frame).start()

    def whole(slot, count, sem):
        part = received.at[slot, pl.ds(0, count)]
        return pltpu.make_async_copy(part, part, sem.at[slot])

    whole(F, N, recv_sem).wait()
    for step in range(F - 1):
        whole(frame_at(step), N - 1, recv_sem).wait()
        own(frame_at(step)).wait()

    slots = [1 + 3 * side, 2 - 2 * side, 3 - 2 * side, 4 - 2 * side]

    @pl.loop(0, N // GROUP)
    def _(index):
        blocks = pl.ds(pl.multiple_of(index * GROUP, GROUP), GROUP)
        out = pl.ds(pl.multiple_of(index * TILE, TILE), TILE)
        seen = [received[slot, blocks].reshape(TILE, C) for slot in slots]
        half = jnp.asarray(0.5, BF16)
        middles = [(seen[k] + seen[k + 1]) * half for k in range(3)]
        for k in range(2):
            even, odd = two_frames(
                middles[k], seen[k + 1], middles[k + 1], seen[k + 2], time_weights, time_bias[...]
            )
            early[2 * k, out] = even
            early[2 * k + 1, out] = odd

    last = frame_at(F - 1)
    for slot in range(F):
        whole(slot, N - 1, send_sem).wait()
    whole(F, N, send_sem).wait()
    whole(last, N - 1, recv_sem).wait()
    own(last).wait()


def exchange(video, spatial_taps, spatial_bias, temporal_taps, temporal_bias):
    return pl.pallas_call(
        exchange_body,
        out_shape=(
            pltpu.VMEM((F + 1, N, BLOCK, C), BF16),
            pltpu.VMEM((F, COUNT, C), BF16),
        ),
        in_specs=[pl.BlockSpec(memory_space=pltpu.HBM)] * 5,
        out_specs=[pl.BlockSpec(memory_space=pltpu.VMEM)] * 2,
        scratch_shapes=[
            pltpu.VMEM((F, R + 2, W, C), BF16),
            pltpu.VMEM((R + 2, W, C), BF16),
            pltpu.VMEM((R + 2, W, C), BF16),
            pltpu.VMEM((F, N, BLOCK, C), BF16),
            pltpu.VMEM((12 * C, 2 * C), BF16),
            pltpu.VMEM((4 * C, 2 * C), BF16),
            pltpu.VMEM((3, 3, C, C), BF16),
            pltpu.VMEM((3, C, C), BF16),
            pltpu.VMEM((1, C), F32),
            pltpu.VMEM((1, C), F32),
            pltpu.SemaphoreType.DMA((F,)),
            pltpu.SemaphoreType.DMA((4,)),
            pltpu.SemaphoreType.DMA((F, 2)),
            pltpu.SemaphoreType.DMA((F, 2)),
            pltpu.SemaphoreType.DMA((F + 1,)),
            pltpu.SemaphoreType.DMA((F + 1,)),
            pltpu.SemaphoreType.DMA((F,)),
        ],
        compiler_params=pltpu.CompilerParams(
            collective_id=0, has_side_effects=True, vmem_limit_bytes=30 * 2**20
        ),
        cost_estimate=pl.CostEstimate(
            flops=2 * 9 * C * C * F * R * W + 3 * C * C * 2 * F * COUNT,
            bytes_accessed=F * R * W * C * 2,
            transcendentals=0,
        ),
        name="spatial_exchange",
    )(
        *(
            pltpu.with_memory_space_constraint(operand, pltpu.HBM)
            for operand in (video, spatial_taps, spatial_bias, temporal_taps, temporal_bias)
        )
    )


def late_body(received, early, taps, bias, doubled, weights, late, early_sem, late_sem):
    side = lax.axis_index("frames")
    copies = [
        pltpu.make_async_copy(early.at[k], doubled.at[F * (1 - side) + k], early_sem.at[k]) for k in range(F)
    ]
    for copy in copies:
        copy.start()
    spread_taps(taps, weights)
    zero, half = jnp.asarray(0.0, BF16), jnp.asarray(0.5, BF16)
    slots = [side, 2 * side, 1 + 2 * side, 2 + side]

    def store(index):
        out = pl.ds(pl.multiple_of(index * TILE, TILE), TILE)
        return pltpu.make_async_copy(
            late.at[:, out], doubled.at[pl.ds(F * side, F), out], late_sem.at[index]
        )

    @pl.loop(0, N // GROUP)
    def _(index):
        blocks = pl.ds(pl.multiple_of(index * GROUP, GROUP), GROUP)
        out = pl.ds(pl.multiple_of(index * TILE, TILE), TILE)
        seen = [received[slot, blocks].reshape(TILE, C) for slot in slots]
        middles = [(seen[k] + seen[k + 1]) * half for k in range(3)]
        middles[0] = jnp.where(side == 0, zero, middles[0])
        middles[2] = jnp.where(side == 0, middles[2], seen[2])
        seen[3] = jnp.where(side == 0, seen[3], zero)
        for k in range(2):
            even, odd = two_frames(
                middles[k], seen[k + 1], middles[k + 1], seen[k + 2], weights, bias[...]
            )
            late[2 * k, out] = even
            late[2 * k + 1, out] = odd
        store(index).start()

    pl.loop(0, N // GROUP)(lambda index: store(index).wait())
    for copy in copies:
        copy.wait()


def finish(received, early, taps, bias):
    return pl.pallas_call(
        late_body,
        out_shape=jax.ShapeDtypeStruct((2 * F, COUNT, C), BF16),
        in_specs=[pl.BlockSpec(memory_space=pltpu.VMEM)] * 4,
        out_specs=pl.BlockSpec(memory_space=pl.ANY),
        scratch_shapes=[
            pltpu.VMEM((4 * C, 2 * C), BF16),
            pltpu.VMEM((F, COUNT, C), BF16),
            pltpu.SemaphoreType.DMA((F,)),
            pltpu.SemaphoreType.DMA((N // GROUP,)),
        ],
        compiler_params=pltpu.CompilerParams(vmem_limit_bytes=16 * 2**20),
        cost_estimate=pl.CostEstimate(
            flops=3 * C * C * 2 * F * COUNT, bytes_accessed=8 * COUNT * C * 2, transcendentals=0
        ),
        name="late_frames",
    )(
        pltpu.with_memory_space_constraint(received, pltpu.VMEM),
        pltpu.with_memory_space_constraint(early, pltpu.VMEM),
        taps,
        bias,
    )


def per_device(video, spatial_kernel, spatial_bias, temporal_kernel, temporal_bias):
    time_bias = temporal_bias.reshape(1, C)
    received, early = exchange(
        video, spatial_kernel, spatial_bias.reshape(1, C), temporal_kernel, time_bias
    )
    doubled = finish(received, early, temporal_kernel, time_bias)
    return doubled.reshape(2 * F, N * R, COLS, C)


def solution(mesh):
    placed = (P("frames", "rows", None, None), P(), P(), P(), P())
    return jax.shard_map(
        per_device,
        mesh=mesh,
        in_specs=placed,
        out_specs=P("frames", None, "rows", None),
        check_vma=False,
    )
```

time: 427 us -> 115 us (0.27)
  blocking collectives: 159 us -> 0 us
  Pallas kernels: 0 us -> 115 us
  local copies, waits for them, and re-layouts: 104 us -> 0.01 us
  matrix products: 67.7 us -> 0 us
  other arithmetic: 43.9 us -> 0 us
  waiting for transfers between devices: 39.5 us -> 0 us
  starting transfers between devices: 11.4 us -> 0 us
    all_to_all x1 -> x0, blocking collectives: 159 us -> none  [per_device(): lax.all_to_all(result, 'rows', split_axis=2, concat_axis=1, tiled=True)]
    pallas_call x0 -> x2, Pallas kernels: none -> 115 us  [the longest x1 109 us: exchange(): pl.pallas_call(exchange_body, out_shape=(pltpu.VMEM((F + 1, N, BLOCK, C),...]
    dot_general x3 -> x0, matrix products: 52 us -> none  [temporal_section(): jnp.einsum('thwc,cd->thwd', upsampled[shift:shift + 2 * count], temporal_...]
    ppermute x4 -> x0, waiting for transfers between devices: 39.5 us -> none  [the longest x2 31 us: extended_2(): lax.ppermute(lax.slice_in_dim(block, block.shape[dim] - width, None, axis...]
    convert_element_type x4 -> x0, local copies, waits for them, and re-layouts: 30.4 us -> none  [the longest x3 18.9 us: per_device(): spatial = (spatial + spatial_bias).astype(jnp.bfloat16)]
    another operation x3 -> x0, other arithmetic: 21.5 us -> none  [temporal_section(): jnp.stack([middles, widened[1:]], axis=1)]
    another operation x2 -> x0, local copies, waits for them, and re-layouts: 17.8 us -> none  [temporal_section(): jnp.stack([middles, widened[1:]], axis=1)]
    unnamed x23 -> x4, local copies, waits for them, and re-layouts: 15.8 us -> 0.01 us
  transfers between devices with their start and end apart: 4 -> 0, of which waited for: 4 -> 0; matrix products, arithmetic and copies ran while one was open for 0% -> 0% of each run, Pallas kernels for 0% -> 0%
where the time goes in v2:
time: 115 us
  Pallas kernels  115 us (100%)
    pallas_call x1, Pallas kernels, exchange(): pl.pallas_call(exchange_body, out_shape=(pltpu.VMEM((F + 1, N, BLOCK, C),...  109 us
    pallas_call x1, Pallas kernels, finish(): pl.pallas_call(late_body, out_shape=jax.ShapeDtypeStruct((2 * F, COUNT, C...  5.74 us

profile of v2, /device:TPU:1, one launch (start us, length us, event | category | flops | bytes accessed | tf_op | source)
XLA Modules:
  0.0 115.0 jit_solution(2003984124491598988)
XLA Ops:
  0.0 0.0 copy-start
  0.0 0.0 copy-start.1
  0.0 109.2 %spatial_exchange.1 = (bf16[5,64,96,128]{3,2,1,0:T(8,128)(2,1)S(1)}, bf16[4,6144,128]{2,1,0:T(8,128)(2,1)S(1)}) custom-call(bf16[4,12,512,128]{3,2,1,0:T(8,128)(2,1)} %video.1, bf16[3,3,128,128]{3,2,1,0:T(8,128)(2,1)} %spatial_taps.1, f32[1,128]{1,0:T(1,128)} %bitcast.5, bf16[3,128,128]{2,1,0:T(8,128)(2,1)} %taps.1, f32[1,128]{1,0:T(1,128)} %bitcast.3), custom_call_target="tpu_custom_call" | custom-call | flops 9663676416 | bytes 6291456 | tf_op jit(solution)/shard_map/spatial_exchange/pallas_call | solution.py:222
  109.2 0.0 copy-done
  109.2 0.0 copy-done.1
  109.2 5.7 %late_frames.1 = bf16[8,6144,128]{2,1,0:T(8,128)(2,1)} custom-call(bf16[5,64,96,128]{3,2,1,0:T(8,128)(2,1)S(1)} %get-tuple-element.7.received, bf16[4,6144,128]{2,1,0:T(8,128)(2,1)S(1)} %get-tuple-element.8.early, bf16[3,128,128]{2,1,0:T(8,128)(2,1)S(1)} %copy-done, f32[1,128]{1,0:T(1,128)S(1)} %bitcast.4), custom_call_target="tpu_custom_call" | custom-call | flops 2415919104 | bytes 12582912 | tf_op jit(solution)/shard_map/late_frames/pallas_call | solution.py:306
Async XLA Ops:
  0.0 109.2 %copy-start = (bf16[3,128,128]{2,1,0:T(8,128)(2,1)S(1)}, bf16[3,128,128]{2,1,0:T(8,128)(2,1)}, u32[]{:S(2)}) copy-start(bf16[3,128,128]{2,1,0:T(8,128)(2,1)} %taps.1) | copy-start | bytes 294916
  0.0 109.2 %copy-start.1 = (f32[128]{0:T(128)S(1)}, f32[128]{0:T(128)}, u32[]{:S(2)}) copy-start(f32[128]{0:T(128)} %param.9) | copy-start | bytes 1540

commit v3 on v2

--- a/solution.py
+++ b/solution.py
@@ -13,6 +13,7 @@
 N = 64
 COLS = W // N
 BLOCK = R * COLS
+EDGE = 2 * COLS
 COUNT = N * BLOCK
 GROUP = 8
 TILE = GROUP * BLOCK
@@ -149,9 +150,10 @@
     def own(frame):
         return pltpu.make_async_copy(outgoing.at[frame, me], received.at[frame, me], own_sem.at[frame])
 
-    def send(frame, slot, peer, where):
+    def send(frame, slot, peer, where, start=0, size=BLOCK):
+        part = pl.ds(start, size)
         pltpu.make_async_remote_copy(
-            src_ref=outgoing.at[frame, peer], dst_ref=received.at[slot, me],
+            src_ref=outgoing.at[frame, peer, part], dst_ref=received.at[slot, me, part],
             send_sem=send_sem.at[slot], recv_sem=recv_sem.at[slot],
             device_id=(peer, where), device_id_type=MESH,
         ).start()
@@ -159,7 +161,14 @@
     head = frame_at(0)
     inner(head)
     pl.semaphore_wait(barrier, 2 * N - 1)
-    for step in range(F):
+    for copy in rim_copies(head):
+        copy.start()
+
+    @pl.loop(1, N)
+    def _(index):
+        send(head, head, partner(me, index), side, EDGE, BLOCK - 2 * EDGE)
+
+    for step in range(1, F):
         for copy in rim_copies(frame_at(step)):
             copy.start()
     outer(head)
@@ -168,8 +177,9 @@
     @pl.loop(1, N)
     def _(index):
         peer = partner(me, index)
-        send(head, head, peer, side)
         send(head, F, peer, 1 - side)
+        send(head, head, peer, side, 0, EDGE)
+        send(head, head, peer, side, BLOCK - EDGE, EDGE)
 
     own(head).start()
 
@@ -179,10 +189,18 @@
         inner(frame)
         outer(frame)
 
-        @pl.loop(1, N)
-        def _(index):
-            send(frame, frame, partner(me, index), side)
-
+        def in_order(early):
+            @pl.loop(1, N)
+            def _(index):
+                peer = partner(me, index)
+                near = ((peer // 2) % 4 == 0) | ((peer // 2) % 4 == 3)
+
+                @pl.when(((step < F - 1) | near) if early else ((step == F - 1) & jnp.logical_not(near)))
+                def _():
+                    send(frame, frame, peer, side)
+
+        in_order(True)
+        in_order(False)
         own(frame).start()
 
     def whole(slot, count, sem):

time: 115 us -> 112 us (0.974)
  Pallas kernels: 115 us -> 112 us
    pallas_call x1, Pallas kernels: 109 us -> 106 us  [exchange(): pl.pallas_call(exchange_body, out_shape=(pltpu.VMEM((F + 1, N, BLOCK, C),...]
where the time goes in v3:
time: 112 us
  Pallas kernels  112 us (100%)
    pallas_call x1, Pallas kernels, exchange(): pl.pallas_call(exchange_body, out_shape=(pltpu.VMEM((F + 1, N, BLOCK, C),...  106 us
    pallas_call x1, Pallas kernels, finish(): pl.pallas_call(late_body, out_shape=jax.ShapeDtypeStruct((2 * F, COUNT, C...  5.74 us

profile of v3, /device:TPU:1, one launch (start us, length us, event | category | flops | bytes accessed | tf_op | source)
XLA Modules:
  0.0 112.1 jit_solution(3097074267477721393)
XLA Ops:
  0.0 0.0 copy-start
  0.0 0.0 copy-start.1
  0.0 106.3 %spatial_exchange.1 = (bf16[5,64,96,128]{3,2,1,0:T(8,128)(2,1)S(1)}, bf16[4,6144,128]{2,1,0:T(8,128)(2,1)S(1)}) custom-call(bf16[4,12,512,128]{3,2,1,0:T(8,128)(2,1)} %video.1, bf16[3,3,128,128]{3,2,1,0:T(8,128)(2,1)} %spatial_taps.1, f32[1,128]{1,0:T(1,128)} %bitcast.5, bf16[3,128,128]{2,1,0:T(8,128)(2,1)} %taps.1, f32[1,128]{1,0:T(1,128)} %bitcast.3), custom_call_target="tpu_custom_call" | custom-call | flops 9663676416 | bytes 6291456 | tf_op jit(solution)/shard_map/spatial_exchange/pallas_call | solution.py:240
  106.3 0.0 copy-done
  106.4 0.0 copy-done.1
  106.4 5.7 %late_frames.1 = bf16[8,6144,128]{2,1,0:T(8,128)(2,1)} custom-call(bf16[5,64,96,128]{3,2,1,0:T(8,128)(2,1)S(1)} %get-tuple-element.7.received, bf16[4,6144,128]{2,1,0:T(8,128)(2,1)S(1)} %get-tuple-element.8.early, bf16[3,128,128]{2,1,0:T(8,128)(2,1)S(1)} %copy-done, f32[1,128]{1,0:T(1,128)S(1)} %bitcast.4), custom_call_target="tpu_custom_call" | custom-call | flops 2415919104 | bytes 12582912 | tf_op jit(solution)/shard_map/late_frames/pallas_call | solution.py:324
Async XLA Ops:
  0.0 106.3 %copy-start = (bf16[3,128,128]{2,1,0:T(8,128)(2,1)S(1)}, bf16[3,128,128]{2,1,0:T(8,128)(2,1)}, u32[]{:S(2)}) copy-start(bf16[3,128,128]{2,1,0:T(8,128)(2,1)} %taps.1) | copy-start | bytes 294916
  0.0 106.4 %copy-start.1 = (f32[128]{0:T(128)S(1)}, f32[128]{0:T(128)}, u32[]{:S(2)}) copy-start(f32[128]{0:T(128)} %param.9) | copy-start | bytes 1540

commit v4 on v3

--- a/solution.py
+++ b/solution.py
@@ -72,9 +72,9 @@
     for copy in small:
         copy.start()
 
-    @pl.loop(1, N, unroll=9)
+    @pl.loop(1, N, unroll=63)
     def _(step):
-        peer = lax.rem(me + step, N)
+        peer = me + step - N * ((me + step) // N)
         pl.semaphore_signal(barrier, inc=1, device_id=(peer, side), device_id_type=MESH)
         pl.semaphore_signal(barrier, inc=1, device_id=(peer, 1 - side), device_id_type=MESH)
 

time: 112 us -> 112 us (level)
  no operation moved by 1% of the time
where the time goes in v4:
time: 112 us
  Pallas kernels  112 us (100%)
    pallas_call x1, Pallas kernels, exchange(): pl.pallas_call(exchange_body, out_shape=(pltpu.VMEM((F + 1, N, BLOCK, C),...  106 us
    pallas_call x1, Pallas kernels, finish(): pl.pallas_call(late_body, out_shape=jax.ShapeDtypeStruct((2 * F, COUNT, C...  5.73 us

profile of v4, /device:TPU:1, one launch (start us, length us, event | category | flops | bytes accessed | tf_op | source)
XLA Modules:
  0.0 111.6 jit_solution(10803368167505642667)
XLA Ops:
  0.0 0.0 copy-start
  0.0 0.0 copy-start.1
  0.0 105.8 %spatial_exchange.1 = (bf16[5,64,96,128]{3,2,1,0:T(8,128)(2,1)S(1)}, bf16[4,6144,128]{2,1,0:T(8,128)(2,1)S(1)}) custom-call(bf16[4,12,512,128]{3,2,1,0:T(8,128)(2,1)} %video.1, bf16[3,3,128,128]{3,2,1,0:T(8,128)(2,1)} %spatial_taps.1, f32[1,128]{1,0:T(1,128)} %bitcast.5, bf16[3,128,128]{2,1,0:T(8,128)(2,1)} %taps.1, f32[1,128]{1,0:T(1,128)} %bitcast.3), custom_call_target="tpu_custom_call" | custom-call | flops 9663676416 | bytes 6291456 | tf_op jit(solution)/shard_map/spatial_exchange/pallas_call | solution.py:240
  105.8 0.0 copy-done
  105.8 0.0 copy-done.1
  105.9 5.7 %late_frames.1 = bf16[8,6144,128]{2,1,0:T(8,128)(2,1)} custom-call(bf16[5,64,96,128]{3,2,1,0:T(8,128)(2,1)S(1)} %get-tuple-element.7.received, bf16[4,6144,128]{2,1,0:T(8,128)(2,1)S(1)} %get-tuple-element.8.early, bf16[3,128,128]{2,1,0:T(8,128)(2,1)S(1)} %copy-done, f32[1,128]{1,0:T(1,128)S(1)} %bitcast.4), custom_call_target="tpu_custom_call" | custom-call | flops 2415919104 | bytes 12582912 | tf_op jit(solution)/shard_map/late_frames/pallas_call | solution.py:324
Async XLA Ops:
  0.0 105.8 %copy-start = (bf16[3,128,128]{2,1,0:T(8,128)(2,1)S(1)}, bf16[3,128,128]{2,1,0:T(8,128)(2,1)}, u32[]{:S(2)}) copy-start(bf16[3,128,128]{2,1,0:T(8,128)(2,1)} %taps.1) | copy-start | bytes 294916
  0.0 105.8 %copy-start.1 = (f32[128]{0:T(128)S(1)}, f32[128]{0:T(128)}, u32[]{:S(2)}) copy-start(f32[128]{0:T(128)} %param.9) | copy-start | bytes 1540

commit v5 on v4

--- a/solution.py
+++ b/solution.py
@@ -22,11 +22,11 @@
 
 
 def partner(row, step):
-    mixed = (37 * step + 10 * step * step) % N
-    y = (row // 16 + mixed // 16) % 4
-    z = (row // 8 + mixed) % 2
-    x = (row // 2 + mixed // 4) % 4
-    core = (row + mixed // 2) % 2
+    mixed = (21 * step + 6 * step * step) % N
+    y = (row // 16 + (mixed // 4)) % 4
+    z = (row // 8 + mixed // 16) % 2
+    x = (row // 2 + (mixed)) % 4
+    core = (row + mixed // 32) % 2
     return ((y * 2 + z) * 4 + x) * 2 + core
 
 

time: 112 us -> 113 us (level); the launches traced: 112 us -> 111 us
  no operation moved by 1% of the time
where the time goes in v5:
time: 113 us; the launch traced here: 111 us
  Pallas kernels  111 us (98%)
    pallas_call x1, Pallas kernels, exchange(): pl.pallas_call(exchange_body, out_shape=(pltpu.VMEM((F + 1, N, BLOCK, C),...  105 us
    pallas_call x1, Pallas kernels, finish(): pl.pallas_call(late_body, out_shape=jax.ShapeDtypeStruct((2 * F, COUNT, C...  5.73 us

profile of v5, /device:TPU:1, one launch (start us, length us, event | category | flops | bytes accessed | tf_op | source)
XLA Modules:
  0.0 110.8 jit_solution(3819967117539991549)
XLA Ops:
  0.0 0.0 copy-start
  0.0 0.0 copy-start.1
  0.0 105.1 %spatial_exchange.1 = (bf16[5,64,96,128]{3,2,1,0:T(8,128)(2,1)S(1)}, bf16[4,6144,128]{2,1,0:T(8,128)(2,1)S(1)}) custom-call(bf16[4,12,512,128]{3,2,1,0:T(8,128)(2,1)} %video.1, bf16[3,3,128,128]{3,2,1,0:T(8,128)(2,1)} %spatial_taps.1, f32[1,128]{1,0:T(1,128)} %bitcast.5, bf16[3,128,128]{2,1,0:T(8,128)(2,1)} %taps.1, f32[1,128]{1,0:T(1,128)} %bitcast.3), custom_call_target="tpu_custom_call" | custom-call | flops 9663676416 | bytes 6291456 | tf_op jit(solution)/shard_map/spatial_exchange/pallas_call | solution.py:240
  105.1 0.0 copy-done
  105.1 0.0 copy-done.1
  105.1 5.7 %late_frames.1 = bf16[8,6144,128]{2,1,0:T(8,128)(2,1)} custom-call(bf16[5,64,96,128]{3,2,1,0:T(8,128)(2,1)S(1)} %get-tuple-element.7.received, bf16[4,6144,128]{2,1,0:T(8,128)(2,1)S(1)} %get-tuple-element.8.early, bf16[3,128,128]{2,1,0:T(8,128)(2,1)S(1)} %copy-done, f32[1,128]{1,0:T(1,128)S(1)} %bitcast.4), custom_call_target="tpu_custom_call" | custom-call | flops 2415919104 | bytes 12582912 | tf_op jit(solution)/shard_map/late_frames/pallas_call | solution.py:324
Async XLA Ops:
  0.0 105.1 %copy-start = (bf16[3,128,128]{2,1,0:T(8,128)(2,1)S(1)}, bf16[3,128,128]{2,1,0:T(8,128)(2,1)}, u32[]{:S(2)}) copy-start(bf16[3,128,128]{2,1,0:T(8,128)(2,1)} %taps.1) | copy-start | bytes 294916
  0.0 105.1 %copy-start.1 = (f32[128]{0:T(128)S(1)}, f32[128]{0:T(128)}, u32[]{:S(2)}) copy-start(f32[128]{0:T(128)} %param.9) | copy-start | bytes 1540
